TPU v7x, 32 devices: a whole 2x2x4 slice. The times are simulated.
32 devices in a mesh: rep: 2 (over core), dp: 8 (over z, y), tensor: 2 (over x).
Axes of the slice: x: 2, y: 2, z: 4, core: 2. Of those that a mesh axis runs over, the one named last changes fastest.
Arguments:
- hidden_in: bfloat16 [8192, 8192], P(('rep', 'dp', 'tensor')), may hold values from -6 to 6
- queries: bfloat16 [8192, 8192], P(('rep', 'dp'), 'tensor'), may hold values from -6 to 6
- keys: bfloat16 [8192, 1024], P(('rep', 'dp'), 'tensor'), may hold values from -6 to 6
- values: bfloat16 [8192, 1024], P(('rep', 'dp'), 'tensor'), may hold values from -6 to 6
- out_grad: bfloat16 [8192, 8192], P(('rep', 'dp'), 'tensor'), may hold values from -6 to 6
- w_key: bfloat16 [8192, 1024], P('dp', 'tensor'), may hold values from -0.0625 to 0.0625
- w_value: bfloat16 [8192, 1024], P('dp', 'tensor'), may hold values from -0.0625 to 0.0625
- adam_state: float32 [2, 2, 8192, 1024], P(None, None, ('rep', 'dp'), 'tensor'), may hold values from -6 to 6
Outputs:
- query_grad: bfloat16 [8192, 8192], P(('rep', 'dp'), 'tensor')
- input_grad: bfloat16 [8192, 8192], P(('rep', 'dp', 'tensor'))
- key_weight_grad: float32 [8192, 1024], P(('rep', 'dp'), 'tensor')
- value_weight_grad: float32 [8192, 1024], P(('rep', 'dp'), 'tensor')
- state_backup: float32 [2, 2, 8192, 1024], P(None, None, ('rep', 'dp'), 'tensor')
All inputs are finite; a program needn't handle non-finite values.
Results may differ from a plain program's by a relative error of at most 0.015.
Values may be sent and summed in bfloat16 or wider, within the bound.
A program may use at most 256 MiB of HBM per device.

v0:
```python
import math

import jax
import jax.numpy as jnp
from jax import lax
from jax.sharding import PartitionSpec as P

HEADS = 64
KVH = 8
HD = 128


def partner(block, axis, apart):
    count = lax.axis_size(axis)
    route = []
    for low in range(count):
        high = low | 1 << apart
        if high != low and high < count:
            route += [(low, high), (high, low)]
    return lax.ppermute(block, axis, route)


def rope_tables(seq_len):
    positions = jnp.arange(seq_len).astype(jnp.float32)
    half_dim = HD // 2
    exponents = jnp.arange(half_dim).astype(jnp.float32) * (2.0 / HD)
    frequency = jnp.exp(-math.log(1000000.0) * exponents)
    angles = positions[:, None] * frequency[None, :]
    return (jnp.cos(angles), jnp.sin(angles))


def unrotate(gradient, cosine, sine_table):
    half_dim = HD // 2
    first_half = gradient[..., :half_dim]
    second_half = gradient[..., half_dim:]
    cos_wide = cosine[:, None, :]
    sin_wide = sine_table[:, None, :]
    return jnp.concatenate(
        [
            first_half * cos_wide + second_half * sin_wide,
            second_half * cos_wide - first_half * sin_wide,
        ],
        axis=-1,
    )


def attention_grads(queries, keys, values, out_grad):
    seq_len = queries.shape[0]
    kv_local = keys.shape[1] // HD
    per_group = HEADS // KVH
    softmax_scale = 1.0 / math.sqrt(HD)
    block_rows = min(seq_len, 512)
    query_heads = queries.reshape(seq_len, kv_local, per_group, HD)
    grad_heads = out_grad.reshape(seq_len, kv_local, per_group, HD)
    key_heads = keys.reshape(seq_len, kv_local, HD)
    value_heads = values.reshape(seq_len, kv_local, HD)
    key_positions = jnp.arange(seq_len)

    def block_step(totals, block_index):
        key_total, value_total = totals
        row_start = block_index * block_rows
        scores = (
            jnp.einsum("qkgd,pkd->kgqp", query_heads, key_heads, preferred_element_type=jnp.float32)
            * softmax_scale
        )
        query_positions = row_start + jnp.arange(block_rows)
        allowed = key_positions[None, :] <= query_positions[:, None]
        scores = jnp.where(allowed, scores, -jnp.inf)
        row_top = jnp.max(scores, axis=-1, keepdims=True)
        weights = jnp.exp(scores - row_top)
        probabilities = weights / jnp.sum(weights, axis=-1, keepdims=True)
        probs_low = probabilities.astype(jnp.bfloat16)
        dprobs = jnp.einsum(
            "qkgd,pkd->kgqp", grad_heads, value_heads, preferred_element_type=jnp.float32
        )
        delta = jnp.sum(probabilities * dprobs, axis=-1, keepdims=True)
        dscores = (probabilities * (dprobs - delta) * softmax_scale).astype(jnp.bfloat16)
        query_block_grad = jnp.einsum(
            "kgqp,pkd->qkgd", dscores, key_heads, preferred_element_type=jnp.float32
        )
        key_total = key_total + jnp.einsum(
            "kgqp,qkgd->pkd", dscores, query_heads, preferred_element_type=jnp.float32
        )
        value_total = value_total + jnp.einsum(
            "kgqp,qkgd->pkd", probs_low, grad_heads, preferred_element_type=jnp.float32
        )
        return ((key_total, value_total), query_block_grad.astype(jnp.bfloat16))

    empty = jnp.zeros((seq_len, kv_local, HD), jnp.float32)
    totals, query_blocks = lax.scan(block_step, (empty, empty), jnp.arange(seq_len // block_rows))
    return (query_blocks.reshape(seq_len, kv_local * per_group * HD), totals[0], totals[1])


def on_device(hidden_in, queries, keys, values, out_grad, w_key, w_value, adam_state):
    state_backup = partner(adam_state, "rep", 0)
    seq_len = queries.shape[0]
    query_grad, rotated_key_grad, value_total = attention_grads(queries, keys, values, out_grad)
    cosine, sine_table = rope_tables(seq_len)
    key_grad = (
        unrotate(rotated_key_grad, cosine, sine_table).reshape(seq_len, -1).astype(jnp.bfloat16)
    )
    value_grad = value_total.reshape(seq_len, -1).astype(jnp.bfloat16)
    local_width = key_grad.shape[1]
    grads_both = jnp.concatenate([key_grad, value_grad], axis=1)
    key_weights, value_weights = (
        lax.all_gather(w_key, "dp", axis=0, tiled=True),
        lax.all_gather(w_value, "dp", axis=0, tiled=True),
    )
    term = lax.dot_general(
        key_grad, key_weights, (((1,), (1,)), ((), ())), preferred_element_type=jnp.float32
    )
    term = term + lax.dot_general(
        value_grad, value_weights, (((1,), (1,)), ((), ())), preferred_element_type=jnp.float32
    )
    input_grad = lax.psum_scatter(
        lax.optimization_barrier(term.astype(jnp.bfloat16))
        .astype(jnp.float32)
        .astype(jnp.bfloat16),
        "tensor",
        scatter_dimension=0,
        tiled=True,
    )
    weight_total = lax.dot_general(
        lax.all_gather(hidden_in, "tensor", axis=0, tiled=True),
        grads_both,
        (((0,), (0,)), ((), ())),
        preferred_element_type=jnp.float32,
    )
    weight_shard = lax.psum_scatter(weight_total, ("rep", "dp"), scatter_dimension=0, tiled=True)
    key_weight_grad = weight_shard[:, :local_width]
    value_weight_grad = weight_shard[:, local_width:]
    return (query_grad, input_grad, key_weight_grad, value_weight_grad, state_backup)


def solution(mesh):
    return jax.shard_map(
        on_device,
        mesh=mesh,
        in_specs=(
            P(("rep", "dp", "tensor"), None),
            P(("rep", "dp"), "tensor"),
            P(("rep", "dp"), "tensor"),
            P(("rep", "dp"), "tensor"),
            P(("rep", "dp"), "tensor"),
            P("dp", "tensor"),
            P("dp", "tensor"),
            P(None, None, ("rep", "dp"), "tensor"),
        ),
        out_specs=(
            P(("rep", "dp"), "tensor"),
            P(("rep", "dp", "tensor"), None),
            P(("rep", "dp"), "tensor"),
            P(("rep", "dp"), "tensor"),
            P(None, None, ("rep", "dp"), "tensor"),
        ),
        check_vma=False,
    )
```

profile of v0, /device:TPU:8, one launch (start us, length us, event | category | flops | bytes accessed | tf_op | source)
XLA Modules:
  0.0 818.8 jit_solution(262793448259341719)
XLA Ops:
  7.2 0.7 all-gather.8.cloned.1.call-update
  8.0 0.7 all-gather.4.cloned.1.call-update
  8.7 0.7 all-gather.6.cloned.1.call-update
  9.4 1.2 reshape.91
  10.9 6.4 copy.41
  17.5 6.7 copy.40
  24.3 0.5 multiply_cosine_fusion
  24.8 15.7 %fusion.27 = f32[4,512,512,8]{2,1,3,0:T(8,128)} fusion(bf16[512,4,8,128]{0,3,2,1:T(8,128)(2,1)} %bitcast.78, bf16[512,4,128,1]{2,1,0,3:T(4,128)(2,1)S(1)} %bitcast.83), kind=kOutput, calls=%fused_computation.31 | convolution fusion | flops 2147483648 | bytes 38273024 | tf_op jit(solution)/shard_map/while/body/eval_jaxpr/qkgd,pkd->kgqp/dot_general | solution.py:73
  40.5 19.0 %fusion.37 = (f32[4,8,512]{2,1,0:T(8,128)S(1)}, f32[4,8,512,512]{2,3,1,0:T(8,128)}) fusion(pred[512,512]{0,1:T(8,128)(4,1)S(1)} %iota_compare_fusion, bf16[512,4,128,1]{0,2,3,1:T(8,128)(2,1)S(1)} %copy.29, bf16[512,4,8,128]{0,3,2,1:T(8,128)(2,1)} %bitcast.80), kind=kOutput, calls=%fused_computation.47 | convolution fusion | flops 2181038592 | bytes 38600704 | tf_op jit(solution)/shard_map/while/body/eval_jaxpr/sub | solution.py:70
  59.5 43.8 %fusion.20 = f32[512,4,128]{0,2,1:T(8,128)S(1)} fusion(bf16[512,4,8,128]{0,3,2,1:T(8,128)(2,1)} %bitcast.81, f32[4,512,512,8]{2,1,3,0:T(8,128)} %fusion.27, f32[4,8,512,512]{2,3,1,0:T(8,128)} %get-tuple-element.44, f32[4,8,512]{2,1,0:T(8,128)S(1)} %get-tuple-element.43), kind=kOutput, calls=%fused_computation.24 | convolution fusion | flops 2206220800 | bytes 72417280 | tf_op jit(solution)/shard_map/while/body/eval_jaxpr/kgqp,qkgd->pkd/dot_general | solution.py:81
  103.5 14.9 %fusion.21 = bf16[4,512,128]{1,2,0:T(8,128)(2,1)S(1)} fusion(bf16[512,4,8,128]{0,3,2,1:T(8,128)(2,1)} %bitcast.79, f32[4,8,512,512]{2,3,1,0:T(8,128)} %get-tuple-element.44, f32[4,8,512]{2,1,0:T(8,128)S(1)} %get-tuple-element.43), kind=kOutput, calls=%fused_computation.25 | convolution fusion | flops 2164523008 | bytes 38338560 | tf_op jit(solution)/shard_map/while/body/eval_jaxpr/kgqp,qkgd->pkd/dot_general | solution.py:84
  118.4 18.5 %convolution_bitcast_fusion = f32[8192,1024]{0,1:T(8,128)} fusion(bf16[512,8192]{1,0:T(8,128)(2,1)} %all-gather.8.cloned.1.call-done, bf16[512,512]{0,1:T(8,128)(2,1)S(1)} %bitcast.87, bf16[512,512]{0,1:T(8,128)(2,1)S(1)} %bitcast.84), kind=kOutput, calls=%fused_computation.10 | convolution fusion | flops 8592031744 | bytes 42991616 | tf_op jit(solution)/shard_map/dot_general | solution.py:123
  137.0 103.1 %all-gather.4.cloned.1.call-done = bf16[8192,512]{1,0:T(8,128)(2,1)} async-done(((bf16[1024,512]{1,0:T(8,128)(2,1)}), bf16[8192,512]{1,0:T(8,128)(2,1)}) %all-gather.4.cloned.1.call-update) | async-done | bytes 8388624 | tf_op jit(solution)/shard_map/all_gather | solution.py:106
  240.1 12.0 %fusion.38 = f32[512,8192]{1,0:T(8,128)} fusion(bf16[512,512]{0,1:T(8,128)(2,1)S(1)} %bitcast.85, bf16[8192,512]{1,0:T(8,128)(2,1)} %all-gather.4.cloned.1.call-done), kind=kOutput, calls=%fused_computation.48 | convolution fusion | flops 4294967296 | bytes 25690112 | tf_op jit(solution)/shard_map/dot_general | solution.py:109
  252.0 113.3 %all-gather.6.cloned.1.call-done = bf16[8192,512]{1,0:T(8,128)(2,1)} async-done(((bf16[1024,512]{1,0:T(8,128)(2,1)}), bf16[8192,512]{1,0:T(8,128)(2,1)}) %all-gather.6.cloned.1.call-update) | async-done | bytes 8388624 | tf_op jit(solution)/shard_map/all_gather | solution.py:107
  365.4 12.9 %add_convert_fusion = bf16[512,8192]{1,0:T(8,128)(2,1)} fusion(f32[512,8192]{1,0:T(8,128)} %fusion.38, bf16[512,512]{0,1:T(8,128)(2,1)S(1)} %bitcast.88, bf16[8192,512]{1,0:T(8,128)(2,1)} %all-gather.6.cloned.1.call-done), kind=kOutput, calls=%fused_computation.11 | convolution fusion | flops 4303355904 | bytes 34078720 | tf_op jit(solution)/shard_map/dot_general | solution.py:112
  378.3 59.9 %fusion.16 = bf16[4,8,512,128]{2,3,1,0:T(8,128)(2,1)} fusion(bf16[512,4,128,1]{0,2,3,1:T(8,128)(2,1)S(1)} %copy.29, f32[4,512,512,8]{2,1,3,0:T(8,128)} %fusion.27, f32[4,8,512,512]{2,3,1,0:T(8,128)} %get-tuple-element.44, f32[4,8,512]{2,1,0:T(8,128)S(1)} %get-tuple-element.43), kind=kOutput, calls=%fused_computation.22 | convolution fusion | flops 2208317952 | bytes 71892992 | tf_op jit(solution)/shard_map/while/body/eval_jaxpr/kgqp,pkd->qkgd/dot_general | solution.py:78
  438.2 6.3 copy.23
  444.5 260.6 %reduce-scatter.5.cloned.1.call-done = f32[512,1024]{0,1:T(8,128)} async-done(((f32[8192,1024]{0,1:T(8,128)}), f32[512,1024]{0,1:T(8,128)}) %reduce-scatter.5.cloned.1.call-update) | async-done | bytes 2097168 | tf_op jit(solution)/shard_map/reduce_scatter | solution.py:129
  705.1 1.7 fusion.36
  706.9 1.3 copy.24
  708.2 1.3 copy.25
  709.5 98.1 %reduce-scatter.3.cloned.1.call-done = bf16[256,8192]{1,0:T(8,128)(2,1)} async-done(((bf16[512,8192]{1,0:T(8,128)(2,1)}), bf16[256,8192]{1,0:T(8,128)(2,1)}) %reduce-scatter.3.cloned.1.call-update) | async-done | bytes 4194320 | tf_op jit(solution)/shard_map/reduce_scatter | solution.py:115
  807.6 4.6 copy.45
  (19 shorter events, 1.1 us)
Async XLA Ops:
  7.2 10.2 %copy-start = (bf16[512,512]{1,0:T(8,128)(2,1)S(1)}, bf16[512,512]{1,0:T(8,128)(2,1)}, u32[]{:S(2)}) copy-start(bf16[512,512]{1,0:T(8,128)(2,1)} %param.11) | copy-start | bytes 1572868
  7.2 111.2 %all-gather.8.cloned.1.call-start = ((), (), s32[]{:S(2)}) async-start(), calls=%async_computation.5 | async-start | bytes 12582912 | tf_op jit(solution)/shard_map/all_gather | solution.py:124
  7.9 232.2 %all-gather.4.cloned.1.call-start = ((), (), s32[]{:S(2)}) async-start(), calls=%async_computation.2 | async-start | bytes 9437184 | tf_op jit(solution)/shard_map/all_gather | solution.py:106
  8.7 356.7 %all-gather.6.cloned.1.call-start = ((), (), s32[]{:S(2)}) async-start(), calls=%async_computation.3 | async-start | bytes 9437184 | tf_op jit(solution)/shard_map/all_gather | solution.py:107
  9.4 695.7 %reduce-scatter.5.cloned.1.call-start = ((), (), s32[]{:S(2)}) async-start(), calls=%async_computation.6 | async-start | bytes 35651584 | tf_op jit(solution)/shard_map/reduce_scatter | solution.py:129
  136.9 670.7 %reduce-scatter.3.cloned.1.call-start = ((), (), s32[]{:S(2)}) async-start(), calls=%async_computation.4 | async-start | bytes 12582912 | tf_op jit(solution)/shard_map/reduce_scatter | solution.py:115
  378.2 66.3 %collective-permute-start = (f32[2,2,512,512]{3,2,1,0:T(8,128)}, f32[2,2,512,512]{3,2,1,0:T(8,128)}, u32[]{:S(2)}, u32[]{:S(2)}) collective-permute-start(f32[2,2,512,512]{3,2,1,0:T(8,128)} %param.15), channel_id=1, source_target_pairs={{0,16},{16,0},{1,17},{17,1},{2,18},{18,2},{3,19},{19,3},{4,20},{20... | collective-permute-start | bytes 12582920 | tf_op jit(solution)/shard_map/ppermute | solution.py:20
Sparse Core Ops, SparseCore 0:
  9.6 105.1 all-gather.7
  116.9 123.1 all-gather.3
  242.2 123.1 all-gather.5
  369.5 335.6 reduce-scatter.4
  707.9 99.7 reduce-scatter.2
where the time goes:
time: 821 us; the launch traced here: 819 us
  waiting for transfers between devices  577 us (70%)
  matrix products  196 us (24%)
  local copies, waits for them, and re-layouts  30 us (4%)
  between operations  13.9 us (2%)
    reduce_scatter x1, waiting for transfers between devices, on_device(): lax.psum_scatter(weight_total, ('rep', 'dp'), scatter_dimension=0, tiled=...  261 us
    all_gather x1, waiting for transfers between devices, on_device(): lax.all_gather(w_value, 'dp', axis=0, tiled=True)  113 us
    all_gather x1, waiting for transfers between devices, on_device(): lax.all_gather(w_key, 'dp', axis=0, tiled=True)  103 us
    reduce_scatter x1, waiting for transfers between devices, on_device(): lax.psum_scatter(lax.optimization_barrier(term.astype(jnp.bfloat16)).asty...  98.1 us
    dot_general x1, matrix products, block_step(): jnp.einsum('kgqp,pkd->qkgd', dscores, key_heads, preferred_element_type=j...  59.9 us
    dot_general x1, matrix products, block_step(): jnp.einsum('kgqp,qkgd->pkd', dscores, query_heads, preferred_element_type...  43.8 us
    sub x1, matrix products, block_step(): weights = jnp.exp(scores - row_top)  19 us
    dot_general x1, matrix products, on_device(): lax.dot_general(lax.all_gather(hidden_in, 'tensor', axis=0, tiled=True),...  18.5 us
  transfers between devices with their start and end apart: 6, of which 4 were waited for; matrix products, arithmetic and copies ran while one was open for 27% of the time, Pallas kernels for 0%

commit v1 on v0

v1 whole, which is shorter than its diff:
```python
import functools
import math

import jax
import jax.numpy as jnp
import numpy as np
from jax import lax
from jax.experimental import pallas as pl
from jax.experimental.pallas import tpu as pltpu
from jax.sharding import PartitionSpec as P

HEADS = 64
KVH = 8
HD = 128
GROUP = HEADS // KVH
MESH = pl.DeviceIdType.MESH
F32, BF16 = jnp.float32, jnp.bfloat16
SUB = 512


def dot(a, b, dims):
    return lax.dot_general(a, b, (dims, ((), ())), preferred_element_type=F32)


def rope_tables(seq_len):
    half = HD // 2
    frequency = np.exp(-math.log(1000000.0) * np.arange(half) * (2.0 / HD))
    angles = np.arange(seq_len)[:, None] * frequency[None, :]
    cosine, sine = np.cos(angles), np.sin(angles)
    return (
        jnp.asarray(np.concatenate([cosine, cosine], 1), F32),
        jnp.asarray(np.concatenate([sine, -sine], 1), F32),
    )


def attention_kernel(q_ref, k_ref, v_ref, og_ref, cos_ref, sin_ref, qg_ref, kg_ref, vg_ref, kt_ref, vt_ref, k_sum, v_sum):
    seq = q_ref.shape[0]
    block = min(256, seq)
    scale = 1.0 / math.sqrt(HD)
    k = k_ref[...]
    v = v_ref[...]
    k_turned = k.T
    k_sum[...] = jnp.zeros_like(k_sum)
    v_sum[...] = jnp.zeros_like(v_sum)

    for head in range(GROUP):
        columns = pl.ds(head * HD, HD)
        for at in range(seq // block):
            rows = pl.ds(at * block, block)
            seen = (at + 1) * block
            q = q_ref[rows, columns]
            og = og_ref[rows, columns]
            scores = dot(k[:seen], q, ((1,), (1,)))
            key_at = lax.broadcasted_iota(jnp.int32, scores.shape, 0)
            query_at = lax.broadcasted_iota(jnp.int32, scores.shape, 1) + at * block
            scores = jnp.where(key_at <= query_at, scores, -jnp.inf)
            top = jnp.max(scores, axis=0, keepdims=True)
            weights = jnp.exp2((scores - top) * (scale * math.log2(math.e)))
            probs = weights * (1.0 / jnp.sum(weights, axis=0, keepdims=True))
            dprobs = dot(v[:seen], og, ((1,), (1,)))
            delta = jnp.sum(probs * dprobs, axis=0, keepdims=True)
            dscores = (probs * (dprobs - delta)).astype(BF16)
            turned = dot(k_turned[:, :seen], dscores, ((1,), (0,)))
            qg_ref[rows, columns] = (turned * scale).T.astype(BF16)
            k_sum[pl.ds(0, seen), :] += dot(dscores, q, ((1,), (0,)))
            v_sum[pl.ds(0, seen), :] += dot(probs.astype(BF16), og, ((1,), (0,)))

    r = k_sum[...] * scale
    kg = r * cos_ref[...] + pltpu.roll(r, HD // 2, 1) * sin_ref[...]
    vg = v_sum[...]
    kg_ref[...] = kg.astype(BF16)
    vg_ref[...] = vg.astype(BF16)
    kt_ref[...] = kg.T.astype(BF16)
    vt_ref[...] = vg.T.astype(BF16)


def attention_grads(queries, keys, values, out_grad):
    seq, width = queries.shape
    kv_width = keys.shape[1]
    groups = kv_width // HD
    cosine, sine = rope_tables(seq)
    wide = pl.BlockSpec((seq, GROUP * HD), lambda g: (0, g))
    narrow = pl.BlockSpec((seq, HD), lambda g: (0, g))
    turned = pl.BlockSpec((HD, seq), lambda g: (g, 0))
    table = pl.BlockSpec((seq, HD), lambda g: (0, 0))
    return pl.pallas_call(
        attention_kernel,
        grid=(groups,),
        in_specs=[wide, narrow, narrow, wide, table, table],
        out_specs=[wide, narrow, narrow, turned, turned],
        out_shape=[
            jax.ShapeDtypeStruct((seq, width), BF16),
            jax.ShapeDtypeStruct((seq, kv_width), BF16),
            jax.ShapeDtypeStruct((seq, kv_width), BF16),
            jax.ShapeDtypeStruct((kv_width, seq), BF16),
            jax.ShapeDtypeStruct((kv_width, seq), BF16),
        ],
        scratch_shapes=[pltpu.VMEM((seq, HD), F32), pltpu.VMEM((seq, HD), F32)],
        compiler_params=pltpu.CompilerParams(vmem_limit_bytes=40 * 2**20),
        cost_estimate=pl.CostEstimate(
            flops=10 * seq * seq * width,
            bytes_accessed=2 * (3 * seq * width + 6 * seq * kv_width),
            transcendentals=seq * seq * width // HD,
        ),
    )(queries, keys, values, out_grad, cosine, sine)


def tail_kernel(
    n_dp, n_tensor,
    kg_ref, vg_ref, kt_ref, vt_ref, hid_ref, w_ref,
    ig_ref, kw_ref, vw_ref, w_other,
    w_slots, hid_slots, ig_send, ig_recv, ig_own, a_send, a_recv, y_send, y_own, y_recv, z_recv, stage,
    w_sem, hid_sem, out_sem, wx_send_sem, wx_recv_sem, ig_send_sem, ig_recv_sem,
    a_send_sem, a_recv_sem, y_send_sem, y_recv_sem, z_send_sem, z_recv_sem,
):
    seq, width = kg_ref.shape
    model = hid_ref.shape[1]
    steps = n_dp // 2
    chunk = model // steps
    part = model // (2 * n_dp)
    sub = min(SUB, chunk)
    piece = seq // n_tensor
    r, d, t = lax.axis_index("rep"), lax.axis_index("dp"), lax.axis_index("tensor")
    a, b = d // 2, d % 2
    partner = {"rep": 1 - r}
    beside = {"dp": a * 2 + (1 - b)}

    def along(k):
        return {"dp": lax.rem(a + 1 + k, steps) * 2 + b}

    def across(k):
        return {"tensor": lax.rem(t + 1 + k, n_tensor)}

    peers = [partner, beside] + [along(k) for k in range(steps - 1)] + [across(k) for k in range(n_tensor - 1)]
    barrier = pltpu.get_barrier_semaphore()
    for peer in peers:
        pl.semaphore_signal(barrier, inc=1, device_id=peer, device_id_type=MESH)

    def send(src, dst, send_sem, recv_sem, peer):
        return pltpu.make_async_remote_copy(
            src_ref=src, dst_ref=dst, send_sem=send_sem, recv_sem=recv_sem, device_id=peer, device_id_type=MESH
        )

    def w_rows(i):
        return pl.ds(i * chunk, chunk)

    w_own = [pltpu.make_async_copy(w_ref.at[w_rows(i)], w_slots.at[i % 2, r], w_sem.at[0, i]) for i in range(steps)]
    w_got = [
        pltpu.make_async_copy(w_other.at[w_rows(i)], w_slots.at[i % 2, 1 - r], w_sem.at[1, i]) for i in range(steps)
    ]
    w_swap = [
        send(w_ref.at[w_rows(i)], w_other.at[w_rows(i)], wx_send_sem.at[i], wx_recv_sem.at[i], partner)
        for i in range(steps)
    ]

    def hid_copy(mine, i):
        owner = r if mine else 1 - r
        first = (owner * n_dp + lax.rem(a + 1 + i, steps) * 2) * part
        columns = pl.ds(pl.multiple_of(first, 2 * part), 2 * part)
        slot = int(mine)
        return pltpu.make_async_copy(hid_ref.at[:, columns], hid_slots.at[slot, i % 2], hid_sem.at[slot, i])

    hid_other = [hid_copy(False, i) for i in range(steps)]
    hid_mine = [hid_copy(True, i) for i in range(steps)]

    def a_copy(i):
        return send(a_send.at[i % 2], a_recv.at[i], a_send_sem.at[i], a_recv_sem.at[i], partner)

    def y_copy(i):
        return send(y_send.at[i], y_recv.at[i], y_send_sem.at[i], y_recv_sem.at[i], beside)

    def z_copy(i):
        return send(y_own.at[i], z_recv.at[i], z_send_sem.at[i], z_recv_sem.at[i], along(i))

    def ig_copy(i, k):
        return send(ig_send.at[k, i], ig_recv.at[k, i], ig_send_sem.at[k, i], ig_recv_sem.at[k, i], across(k))

    def turned_product(which, slot, which_b, half):
        turned = kt_ref if half == 0 else vt_ref
        columns = pl.ds(pl.multiple_of(which_b * part, part), part)
        return dot(turned[...], hid_slots[which, slot, :, columns], ((1,), (0,)))

    def input_grads(i):
        for s in range(chunk // sub):
            columns = pl.ds(s * sub, sub)
            total = dot(kg_ref[...], w_slots[i % 2, 0, columns, :], ((1,), (1,)))
            total = total + dot(vg_ref[...], w_slots[i % 2, 1, columns, :], ((1,), (1,)))
            stage[...] = total.astype(BF16)
            for k in range(n_tensor - 1):
                first = pl.multiple_of(lax.rem(t + 1 + k, n_tensor) * piece, piece)
                ig_send[k, i, :, columns] = stage[pl.ds(first, piece), :]
            ig_own[i, :, columns] = stage[pl.ds(pl.multiple_of(t * piece, piece), piece), :]

    def other_products(i):
        for which_b in range(2):
            for half in range(2):
                out = pl.ds(half * width, width)
                a_send[i % 2, which_b, out, :] = turned_product(0, i % 2, which_b, half).astype(BF16)

    def own_products(i, which_b, into):
        for half in range(2):
            out = pl.ds(half * width, width)
            total = turned_product(1, i % 2, which_b, half) + a_recv[i, which_b, out, :].astype(F32)
            into[i, out, :] = total.astype(BF16)

    w_own[0].start()
    hid_other[0].start()
    hid_mine[0].start()
    pl.semaphore_wait(barrier, len(peers))
    w_swap[0].start()

    for i in range(steps + 2):
        if i < steps:
            hid_other[i].wait()
            if i >= 2:
                a_copy(i - 2).wait_send()
            other_products(i)
            a_copy(i).start()
            if i + 1 < steps:
                w_swap[i + 1].start()
                hid_other[i + 1].start()
                w_own[i + 1].start()
            w_swap[i].wait_recv()
            w_got[i].start()
            w_got[i].wait()
            w_own[i].wait()
            input_grads(i)
            for k in range(n_tensor - 1):
                ig_copy(i, k).start()
        if 1 <= i <= steps:
            done = i - 1
            if i < steps:
                hid_mine[i].start()
            hid_mine[done].wait()
            a_copy(done).wait_recv()
            own_products(done, 1 - b, y_send)
            y_copy(done).start()
            own_products(done, b, y_own)
        if i >= 2:
            done = i - 2
            y_copy(done).wait_recv()
            if done < steps - 1:
                y_own[done] = (y_own[done].astype(F32) + y_recv[done].astype(F32)).astype(BF16)
                z_copy(done).start()

    ig_out = []
    for i in range(steps):
        for k in range(n_tensor - 1):
            ig_copy(i, k).wait_recv()
        for s in range(chunk // sub):
            columns = pl.ds(s * sub, sub)
            total = ig_own[i, :, columns].astype(F32)
            for k in range(n_tensor - 1):
                total = total + ig_recv[k, i, :, columns].astype(F32)
            ig_own[i, :, columns] = total.astype(BF16)
        copy = pltpu.make_async_copy(ig_own.at[i], ig_ref.at[:, pl.ds(i * chunk, chunk)], out_sem.at[i])
        copy.start()
        ig_out.append(copy)

    for k in range(steps - 1):
        z_copy(k).wait_recv()
    for half, out_ref in enumerate((kw_ref, vw_ref)):
        out = pl.ds(half * width, width)
        total = y_own[steps - 1, out, :].astype(F32) + y_recv[steps - 1, out, :].astype(F32)
        for k in range(steps - 1):
            total = total + z_recv[k, out, :].astype(F32)
        out_ref[...] = total.T

    for i in range(steps):
        w_swap[i].wait_send()
        y_copy(i).wait_send()
        if i < steps - 1:
            z_copy(i).wait_send()
        if i >= steps - 2:
            a_copy(i).wait_send()
        for k in range(n_tensor - 1):
            ig_copy(i, k).wait_send()
        ig_out[i].wait()


def tail(mesh, kg, vg, kt, vt, hid, w_half):
    n_dp, n_tensor = mesh.shape["dp"], mesh.shape["tensor"]
    seq, width = kg.shape
    model = hid.shape[1]
    steps = n_dp // 2
    chunk = model // steps
    part = model // (2 * n_dp)
    piece = seq // n_tensor
    others = n_tensor - 1
    sems = pltpu.SemaphoreType.DMA
    vmem = pl.BlockSpec(memory_space=pltpu.VMEM)
    anywhere = pl.BlockSpec(memory_space=pl.ANY)
    return pl.pallas_call(
        functools.partial(tail_kernel, n_dp, n_tensor),
        in_specs=[vmem, vmem, vmem, vmem, anywhere, anywhere],
        out_specs=[anywhere, vmem, vmem, anywhere],
        out_shape=[
            jax.ShapeDtypeStruct((piece, model), BF16),
            jax.ShapeDtypeStruct((part, width), F32),
            jax.ShapeDtypeStruct((part, width), F32),
            jax.ShapeDtypeStruct((model, width), BF16),
        ],
        scratch_shapes=[
            pltpu.VMEM((2, 2, chunk, width), BF16),
            pltpu.VMEM((2, 2, seq, 2 * part), BF16),
            pltpu.VMEM((others, steps, piece, chunk), BF16),
            pltpu.VMEM((others, steps, piece, chunk), BF16),
            pltpu.VMEM((steps, piece, chunk), BF16),
            pltpu.VMEM((2, 2, 2 * width, part), BF16),
            pltpu.VMEM((steps, 2, 2 * width, part), BF16),
            pltpu.VMEM((steps, 2 * width, part), BF16),
            pltpu.VMEM((steps, 2 * width, part), BF16),
            pltpu.VMEM((steps, 2 * width, part), BF16),
            pltpu.VMEM((steps - 1, 2 * width, part), BF16),
            pltpu.VMEM((seq, min(SUB, chunk)), BF16),
            sems((2, steps)),
            sems((2, steps)),
            sems((steps,)),
            sems((steps,)),
            sems((steps,)),
            sems((others, steps)),
            sems((others, steps)),
            sems((steps,)),
            sems((steps,)),
            sems((steps,)),
            sems((steps,)),
            sems((steps - 1,)),
            sems((steps - 1,)),
        ],
        compiler_params=pltpu.CompilerParams(
            collective_id=0, has_side_effects=True, vmem_limit_bytes=62 * 2**20
        ),
        cost_estimate=pl.CostEstimate(
            flops=8 * seq * width * model, bytes_accessed=8 * model * width, transcendentals=0
        ),
    )(kg, vg, kt, vt, hid, w_half)[:3]


def on_device(mesh, hidden_in, queries, keys, values, out_grad, w_key, w_value, adam_state):
    state_backup = lax.ppermute(adam_state, "rep", [(0, 1), (1, 0)])
    hidden = lax.all_gather(hidden_in, "tensor", axis=0, tiled=True)
    w_mine = jnp.where(lax.axis_index("rep") == 0, w_key, w_value)
    w_half = lax.all_gather(w_mine, "dp", axis=0, tiled=True)
    query_grad, kg, vg, kt, vt = attention_grads(queries, keys, values, out_grad)
    input_grad, key_weight_grad, value_weight_grad = tail(mesh, kg, vg, kt, vt, hidden, w_half)
    return (query_grad, input_grad, key_weight_grad, value_weight_grad, state_backup)


def solution(mesh):
    return jax.shard_map(
        functools.partial(on_device, mesh),
        mesh=mesh,
        in_specs=(
            P(("rep", "dp", "tensor"), None),
            P(("rep", "dp"), "tensor"),
            P(("rep", "dp"), "tensor"),
            P(("rep", "dp"), "tensor"),
            P(("rep", "dp"), "tensor"),
            P("dp", "tensor"),
            P("dp", "tensor"),
            P(None, None, ("rep", "dp"), "tensor"),
        ),
        out_specs=(
            P(("rep", "dp"), "tensor"),
            P(("rep", "dp", "tensor"), None),
            P(("rep", "dp"), "tensor"),
            P(("rep", "dp"), "tensor"),
            P(None, None, ("rep", "dp"), "tensor"),
        ),
        check_vma=False,
    )
```

time: 821 us -> 399 us (0.49)
  waiting for transfers between devices: 577 us -> 186 us
  matrix products: 196 us -> 0 us
  Pallas kernels: 0 us -> 176 us
  local copies, waits for them, and re-layouts: 30 us -> 19.4 us
    reduce_scatter x2 -> x0, waiting for transfers between devices: 359 us -> none  [the longest x1 261 us: on_device(): lax.psum_scatter(weight_total, ('rep', 'dp'), scatter_dimension=0, tiled=...]
    dot_general x7 -> x0, matrix products: 177 us -> none  [the longest x1 59.9 us: block_step(): jnp.einsum('kgqp,pkd->qkgd', dscores, key_heads, preferred_element_type=j...]
    pallas_call x0 -> x2, Pallas kernels: none -> 176 us  [the longest x1 139 us: tail(): pl.pallas_call(functools.partial(tail_kernel, n_dp, n_tensor), in_specs=[...]
    all_gather x3 -> x2, waiting for transfers between devices: 216 us -> 186 us  [the longest x1 126 us: on_device(): w_half = lax.all_gather(w_mine, 'dp', axis=0, tiled=True)]
    sub x1 -> x0, matrix products: 19 us -> none  [block_step(): weights = jnp.exp(scores - row_top)]
    reshape x5 -> x0, local copies, waits for them, and re-layouts: 14.7 us -> none  [the longest x1 6.71 us: attention_grads(): query_heads = queries.reshape(seq_len, kv_local, per_group, HD)]
    unnamed x6 -> x30, local copies, waits for them, and re-layouts: 13.6 us -> 19.4 us
  transfers between devices with their start and end apart: 6 -> 3, of which waited for: 4 -> 2; matrix products, arithmetic and copies ran while one was open for 27% -> 0% of each run, Pallas kernels for 0% -> 9%
where the time goes in v1:
time: 399 us; the launch traced here: 398 us
  waiting for transfers between devices  186 us (47%)
  Pallas kernels  176 us (44%)
  local copies, waits for them, and re-layouts  19.4 us (5%)
  between operations  14.1 us (4%)
    pallas_call x1, Pallas kernels, tail(): pl.pallas_call(functools.partial(tail_kernel, n_dp, n_tensor), in_specs=[...  139 us
    all_gather x1, waiting for transfers between devices, on_device(): w_half = lax.all_gather(w_mine, 'dp', axis=0, tiled=True)  126 us
    all_gather x1, waiting for transfers between devices, on_device(): hidden = lax.all_gather(hidden_in, 'tensor', axis=0, tiled=True)  59.8 us
    pallas_call x1, Pallas kernels, attention_grads(): pl.pallas_call(attention_kernel, grid=(groups,), in_specs=[wide, narrow,...  36.7 us
    unnamed x30, local copies, waits for them, and re-layouts  19.4 us
  transfers between devices with their start and end apart: 3, of which 2 were waited for; matrix products, arithmetic and copies ran while one was open for 0% of the time, Pallas kernels for 9%

profile of v1, /device:TPU:8, one launch (start us, length us, event | category | flops | bytes accessed | tf_op | source)
XLA Modules:
  0.0 397.8 jit_solution(5087051564913496724)
XLA Ops:
  7.2 0.0 copy-start.4
  7.2 0.0 copy-start.5
  7.2 0.0 all-gather.3.cloned.1.call-start
  7.3 0.7 all-gather.3.cloned.1.call-update
  8.0 0.0 all-gather.5.cloned.1.call-start
  8.0 0.5 copy-done.10
  8.5 1.1 broadcast_select_fusion
  9.6 0.0 all-gather.5.cloned.1.call-update
  9.6 1.1 collective-permute-start
  10.7 0.0 copy-start
  10.7 2.2 copy-done
  12.9 2.2 copy-done.1
  15.1 36.7 %shard_map.137 = (bf16[512,4096]{1,0:T(8,128)(2,1)}, bf16[512,512]{1,0:T(8,128)(2,1)S(1)}, bf16[512,512]{1,0:T(8,128)(2,1)S(1)}, bf16[512,512]{1,0:T(8,128)(2,1)S(1)}, bf16[512,512]{1,0:T(8,128)(2,1)S(1)}) custom-call(bf16[512,4096]{1,0:T(8,128)(2,1)S(1)} %copy-done, bf16[512,512]{1,0:T(8,128)(2,1)S(1)} %copy-done.2, bf16[512,512]{1,0:T(8,128)(2,1)S(1)} %copy-done.3, ...), custom_call_target="tpu_custom_call" | custom-call | flops 10737418240 | bytes 15728640 | tf_op jit(solution)/shard_map/pallas_call | solution.py:86
  51.8 0.8 copy-done.6
  52.6 0.8 copy-done.7
  53.4 0.8 copy-done.8
  54.2 0.8 copy-done.9
  55.0 59.8 %all-gather.3.cloned.1.call-done.hid_ref = bf16[512,8192]{1,0:T(8,128)(2,1)} async-done(((bf16[256,8192]{1,0:T(8,128)(2,1)}), bf16[512,8192]{1,0:T(8,128)(2,1)}) %all-gather.3.cloned.1.call-update) | async-done | bytes 8388624 | tf_op jit(solution)/shard_map/all_gather | solution.py:341
  114.8 125.8 %all-gather.5.cloned.1.call-done.w_ref = bf16[8192,512]{1,0:T(8,128)(2,1)} async-done(((bf16[1024,512]{1,0:T(8,128)(2,1)}), bf16[8192,512]{1,0:T(8,128)(2,1)}) %all-gather.5.cloned.1.call-update) | async-done | bytes 8388624 | tf_op jit(solution)/shard_map/all_gather | solution.py:343
  240.6 138.9 %shard_map.138 = (bf16[256,8192]{1,0:T(8,128)(2,1)}, f32[512,512]{1,0:T(8,128)}, f32[512,512]{1,0:T(8,128)}, bf16[8192,512]{1,0:T(8,128)(2,1)}) custom-call(bf16[512,512]{1,0:T(8,128)(2,1)} %copy-done.6, bf16[512,512]{1,0:T(8,128)(2,1)} %copy-done.7, bf16[512,512]{1,0:T(8,128)(2,1)} %copy-done.8, bf16[512,512]{1,0:T(8,128)(2,1)} %copy-done.9, ...), custom_call_target="tpu_custom_call" | custom-call | flops 17179869184 | bytes 33554432 | tf_op jit(solution)/shard_map/pallas_call | solution.py:293
  379.6 4.8 %copy.19 = bf16[256,8192]{1,0:T(8,128)(2,1)} copy(bf16[256,8192]{1,0:T(8,128)(2,1)} %get-tuple-element.27) | data formatting | bytes 8388608
  384.4 1.0 copy.20
  385.3 1.0 copy.21
  386.3 4.6 %copy.22 = f32[2,2,512,512]{3,2,1,0:T(8,128)} copy(f32[2,2,512,512]{3,2,1,0:T(8,128)} %collective-permute-done) | data formatting | bytes 8388608
  (17 shorter events, 0.0 us)
Async XLA Ops:
  7.2 3.5 copy-start.4
  7.2 3.5 copy-start.5
  7.2 1.3 copy-start.10
  7.2 3.5 copy-start.2
  7.2 3.5 copy-start.3
  7.2 107.6 %all-gather.3.cloned.1.call-start = ((), (), s32[]{:S(2)}) async-start(), calls=%async_computation | async-start | bytes 12582912 | tf_op jit(solution)/shard_map/all_gather | solution.py:341
  8.0 232.7 %all-gather.5.cloned.1.call-start = ((), (), s32[]{:S(2)}) async-start(), calls=%async_computation.1 | async-start | bytes 9437184 | tf_op jit(solution)/shard_map/all_gather | solution.py:343
  9.6 45.4 %collective-permute-start = (f32[2,2,512,512]{3,2,1,0:T(8,128)}, f32[2,2,512,512]{3,2,1,0:T(8,128)}, u32[]{:S(2)}, u32[]{:S(2)}) collective-permute-start(f32[2,2,512,512]{3,2,1,0:T(8,128)} %param.17), channel_id=1, source_target_pairs={{0,16},{16,0},{1,17},{17,1},{2,18},{18,2},{3,19},{19,3},{4,20},{20... | collective-permute-start | bytes 12582920 | tf_op jit(solution)/shard_map/ppermute | solution.py:340
  10.7 2.2 copy-start
  12.9 2.2 copy-start.1
  51.8 0.8 copy-start.6
  52.6 0.8 copy-start.7
  53.4 0.8 copy-start.8
  54.2 0.8 copy-start.9
  379.6 4.8 %copy-start.12 = (f32[512,512]{1,0:T(8,128)S(1)}, f32[512,512]{1,0:T(8,128)}, u32[]{:S(2)}) copy-start(f32[512,512]{1,0:T(8,128)} %get-tuple-element.28) | copy-start | bytes 3145732
  379.6 5.8 %copy-start.11 = (f32[512,512]{1,0:T(8,128)S(1)}, f32[512,512]{1,0:T(8,128)}, u32[]{:S(2)}) copy-start(f32[512,512]{1,0:T(8,128)} %get-tuple-element.29) | copy-start | bytes 3145732
Sparse Core Ops, SparseCore 0:
  9.6 105.1 all-gather.2
  117.5 123.0 all-gather.4

commit v2 on v1

--- a/solution.py
+++ b/solution.py
@@ -96,7 +96,7 @@
             jax.ShapeDtypeStruct((kv_width, seq), BF16),
         ],
         scratch_shapes=[pltpu.VMEM((seq, HD), F32), pltpu.VMEM((seq, HD), F32)],
-        compiler_params=pltpu.CompilerParams(vmem_limit_bytes=40 * 2**20),
+        compiler_params=pltpu.CompilerParams(vmem_limit_bytes=62 * 2**20),
         cost_estimate=pl.CostEstimate(
             flops=10 * seq * seq * width,
             bytes_accessed=2 * (3 * seq * width + 6 * seq * kv_width),
@@ -105,21 +105,33 @@
     )(queries, keys, values, out_grad, cosine, sine)
 
 
+def by_distance(place, count, i):
+    found = 0
+    for here in range(count):
+        near = sorted(range(count), key=lambda other: abs(other - here))
+        found = found + jnp.where(place == here, near[i], 0)
+    return found
+
+
 def tail_kernel(
-    n_dp, n_tensor,
-    kg_ref, vg_ref, kt_ref, vt_ref, hid_ref, w_ref,
-    ig_ref, kw_ref, vw_ref, w_other,
+    n_dp, n_tensor, early,
+    kg_ref, vg_ref, kt_ref, vt_ref, hid_ref, hid_early, w_ref, w_below, w_above, w_beside,
+    ig_ref, kw_ref, vw_ref, w_all, hid_all,
     w_slots, hid_slots, ig_send, ig_recv, ig_own, a_send, a_recv, y_send, y_own, y_recv, z_recv, stage,
-    w_sem, hid_sem, out_sem, wx_send_sem, wx_recv_sem, ig_send_sem, ig_recv_sem,
+    w_sem, hid_sem, in_sem, out_sem,
+    wz_send_sem, wz_recv_sem, wy_send_sem, wy_recv_sem, wr_send_sem, wr_recv_sem,
+    hx_send_sem, hx_recv_sem, ig_send_sem, ig_recv_sem,
     a_send_sem, a_recv_sem, y_send_sem, y_recv_sem, z_send_sem, z_recv_sem,
 ):
     seq, width = kg_ref.shape
     model = hid_ref.shape[1]
     steps = n_dp // 2
     chunk = model // steps
+    shard = model // n_dp
     part = model // (2 * n_dp)
     sub = min(SUB, chunk)
     piece = seq // n_tensor
+    others = n_tensor - 1
     r, d, t = lax.axis_index("rep"), lax.axis_index("dp"), lax.axis_index("tensor")
     a, b = d // 2, d % 2
     partner = {"rep": 1 - r}
@@ -131,7 +143,7 @@
     def across(k):
         return {"tensor": lax.rem(t + 1 + k, n_tensor)}
 
-    peers = [partner, beside] + [along(k) for k in range(steps - 1)] + [across(k) for k in range(n_tensor - 1)]
+    peers = [partner, beside] + [along(k) for k in range(steps - 1)] + [across(k) for k in range(others)]
     barrier = pltpu.get_barrier_semaphore()
     for peer in peers:
         pl.semaphore_signal(barrier, inc=1, device_id=peer, device_id_type=MESH)
@@ -141,27 +153,87 @@
             src_ref=src, dst_ref=dst, send_sem=send_sem, recv_sem=recv_sem, device_id=peer, device_id_type=MESH
         )
 
-    def w_rows(i):
-        return pl.ds(i * chunk, chunk)
-
-    w_own = [pltpu.make_async_copy(w_ref.at[w_rows(i)], w_slots.at[i % 2, r], w_sem.at[0, i]) for i in range(steps)]
-    w_got = [
-        pltpu.make_async_copy(w_other.at[w_rows(i)], w_slots.at[i % 2, 1 - r], w_sem.at[1, i]) for i in range(steps)
-    ]
-    w_swap = [
-        send(w_ref.at[w_rows(i)], w_other.at[w_rows(i)], wx_send_sem.at[i], wx_recv_sem.at[i], partner)
-        for i in range(steps)
-    ]
-
-    def hid_copy(mine, i):
+    near = [by_distance(a, steps, i) for i in range(steps)]
+
+    def w_onward(i):
+        place = near[i]
+        target = jnp.where(place < a, a + 1, a - 1)
+        inside = (target >= 0) & (target < steps)
+        target = jnp.clip(target, 0, steps - 1)
+        slot = w_all.at[r, place, b]
+        return inside, send(slot, slot, wz_send_sem.at[place], wz_recv_sem.at[place], {"dp": target * 2 + b})
+
+    def w_sideways(i):
+        slot = w_all.at[r, near[i], b]
+        return send(slot, slot, wy_send_sem.at[i], wy_recv_sem.at[i], beside)
+
+    def w_swap(i, theirs):
+        which = 1 - b if theirs else b
+        slot = w_all.at[r, near[i], which]
+        return send(slot, slot, wr_send_sem.at[i, int(theirs)], wr_recv_sem.at[i, int(theirs)], partner)
+
+    def w_load(i):
+        return [
+            pltpu.make_async_copy(
+                w_all.at[kind, near[i], which],
+                w_slots.at[i % 2, kind, pl.ds(which * shard, shard)],
+                w_sem.at[i, kind, which],
+            )
+            for kind in range(2)
+            for which in range(2)
+        ]
+
+    def take_line(i):
+        if i >= 1:
+
+            @pl.when(jnp.abs(near[i] - a) >= 2)
+            def _():
+                w_onward(i)[1].wait_recv()
+
+            inside, copy = w_onward(i)
+            pl.when(inside)(copy.start)
+            w_sideways(i).start()
+        w_swap(i, False).start()
+
+    def take_beside(i):
+        if i >= 1:
+            w_sideways(i).wait_recv()
+        w_swap(i, True).start()
+
+    def hid_columns(mine, i):
         owner = r if mine else 1 - r
         first = (owner * n_dp + lax.rem(a + 1 + i, steps) * 2) * part
-        columns = pl.ds(pl.multiple_of(first, 2 * part), 2 * part)
-        slot = int(mine)
-        return pltpu.make_async_copy(hid_ref.at[:, columns], hid_slots.at[slot, i % 2], hid_sem.at[slot, i])
-
-    hid_other = [hid_copy(False, i) for i in range(steps)]
-    hid_mine = [hid_copy(True, i) for i in range(steps)]
+        return pl.ds(pl.multiple_of(first, 2 * part), 2 * part)
+
+    def hid_send(mine, i, k):
+        w = int(mine)
+        return send(
+            hid_ref.at[:, hid_columns(mine, i)], hid_all.at[k, i, w], hx_send_sem.at[k, i, w], hx_recv_sem.at[k, i, w], across(k)
+        )
+
+    def hid_load(mine, i):
+        w = int(mine)
+
+        def rows(owner):
+            return hid_slots.at[w, i % 2, pl.ds(pl.multiple_of(owner * piece, piece), piece)]
+
+        copies = [pltpu.make_async_copy(hid_ref.at[:, hid_columns(mine, i)], rows(t), hid_sem.at[w, i, others])]
+        for k in range(others):
+            source = hid_early.at[k, i, w] if i < early else hid_all.at[k, i, w]
+            owner = lax.rem(t + n_tensor - 1 - k, n_tensor)
+            copies.append(pltpu.make_async_copy(source, rows(owner), hid_sem.at[w, i, k]))
+        return copies
+
+    def hid_start(mine, i):
+        if i >= early:
+            for k in range(others):
+                hid_send(mine, i, k).wait_recv()
+        for copy in hid_load(mine, i):
+            copy.start()
+
+    def hid_wait(mine, i):
+        for copy in hid_load(mine, i):
+            copy.wait()
 
     def a_copy(i):
         return send(a_send.at[i % 2], a_recv.at[i], a_send_sem.at[i], a_recv_sem.at[i], partner)
@@ -203,39 +275,57 @@
             total = turned_product(1, i % 2, which_b, half) + a_recv[i, which_b, out, :].astype(F32)
             into[i, out, :] = total.astype(BF16)
 
-    w_own[0].start()
-    hid_other[0].start()
-    hid_mine[0].start()
+    def enter(index, source, place, which):
+        return pltpu.make_async_copy(source, w_all.at[r, place, which], in_sem.at[index])
+
+    below, above = jnp.maximum(a - 1, 0), jnp.minimum(a + 1, steps - 1)
+    enter(0, w_ref, a, b).start()
+    enter(1, w_beside, a, 1 - b).start()
+    pl.when(a >= 1)(enter(2, w_below, below, b).start)
+    pl.when(a + 1 < steps)(enter(3, w_above, above, b).start)
     pl.semaphore_wait(barrier, len(peers))
-    w_swap[0].start()
+    for i in range(early, steps):
+        for mine in (False, True):
+            for k in range(others):
+                hid_send(mine, i, k).start()
+    enter(0, w_ref, a, b).wait()
+    enter(1, w_beside, a, 1 - b).wait()
+    pl.when(a >= 1)(enter(2, w_below, below, b).wait)
+    pl.when(a + 1 < steps)(enter(3, w_above, above, b).wait)
+    take_line(0)
+    take_beside(0)
+    take_line(1)
 
     for i in range(steps + 2):
         if i < steps:
-            hid_other[i].wait()
+            hid_start(False, i)
+            if i >= 1:
+                take_beside(i)
+                if i + 1 < steps:
+                    take_line(i + 1)
+            hid_wait(False, i)
             if i >= 2:
                 a_copy(i - 2).wait_send()
             other_products(i)
             a_copy(i).start()
-            if i + 1 < steps:
-                w_swap[i + 1].start()
-                hid_other[i + 1].start()
-                w_own[i + 1].start()
-            w_swap[i].wait_recv()
-            w_got[i].start()
-            w_got[i].wait()
-            w_own[i].wait()
-            input_grads(i)
-            for k in range(n_tensor - 1):
-                ig_copy(i, k).start()
+            hid_start(True, i)
+            w_swap(i, False).wait_recv()
+            w_swap(i, True).wait_recv()
+            for copy in w_load(i):
+                copy.start()
         if 1 <= i <= steps:
             done = i - 1
-            if i < steps:
-                hid_mine[i].start()
-            hid_mine[done].wait()
+            hid_wait(True, done)
             a_copy(done).wait_recv()
             own_products(done, 1 - b, y_send)
             y_copy(done).start()
             own_products(done, b, y_own)
+        if i < steps:
+            for copy in w_load(i):
+                copy.wait()
+            input_grads(i)
+            for k in range(others):
+                ig_copy(i, k).start()
         if i >= 2:
             done = i - 2
             y_copy(done).wait_recv()
@@ -253,7 +343,7 @@
             for k in range(n_tensor - 1):
                 total = total + ig_recv[k, i, :, columns].astype(F32)
             ig_own[i, :, columns] = total.astype(BF16)
-        copy = pltpu.make_async_copy(ig_own.at[i], ig_ref.at[:, pl.ds(i * chunk, chunk)], out_sem.at[i])
+        copy = pltpu.make_async_copy(ig_own.at[i], ig_ref.at[:, pl.ds(pl.multiple_of(near[i] * chunk, chunk), chunk)], out_sem.at[i])
         copy.start()
         ig_out.append(copy)
 
@@ -267,7 +357,16 @@
         out_ref[...] = total.T
 
     for i in range(steps):
-        w_swap[i].wait_send()
+        w_swap(i, False).wait_send()
+        w_swap(i, True).wait_send()
+        if i >= 1:
+            inside, copy = w_onward(i)
+            pl.when(inside)(copy.wait_send)
+            w_sideways(i).wait_send()
+        if i >= early:
+            for mine in (False, True):
+                for k in range(others):
+                    hid_send(mine, i, k).wait_send()
         y_copy(i).wait_send()
         if i < steps - 1:
             z_copy(i).wait_send()
@@ -278,12 +377,16 @@
         ig_out[i].wait()
 
 
-def tail(mesh, kg, vg, kt, vt, hid, w_half):
+EARLY = 1
+
+
+def tail(mesh, kg, vg, kt, vt, hidden, hid_early, w_mine, w_below, w_above, w_beside):
     n_dp, n_tensor = mesh.shape["dp"], mesh.shape["tensor"]
     seq, width = kg.shape
-    model = hid.shape[1]
+    model = hidden.shape[1]
     steps = n_dp // 2
     chunk = model // steps
+    shard = model // n_dp
     part = model // (2 * n_dp)
     piece = seq // n_tensor
     others = n_tensor - 1
@@ -291,14 +394,15 @@
     vmem = pl.BlockSpec(memory_space=pltpu.VMEM)
     anywhere = pl.BlockSpec(memory_space=pl.ANY)
     return pl.pallas_call(
-        functools.partial(tail_kernel, n_dp, n_tensor),
-        in_specs=[vmem, vmem, vmem, vmem, anywhere, anywhere],
-        out_specs=[anywhere, vmem, vmem, anywhere],
+        functools.partial(tail_kernel, n_dp, n_tensor, EARLY),
+        in_specs=[vmem] * 4 + [anywhere] * 6,
+        out_specs=[anywhere, vmem, vmem, anywhere, anywhere],
         out_shape=[
             jax.ShapeDtypeStruct((piece, model), BF16),
             jax.ShapeDtypeStruct((part, width), F32),
             jax.ShapeDtypeStruct((part, width), F32),
-            jax.ShapeDtypeStruct((model, width), BF16),
+            jax.ShapeDtypeStruct((2, steps, 2, shard, width), BF16),
+            jax.ShapeDtypeStruct((others, steps, 2, piece, 2 * part), BF16),
         ],
         scratch_shapes=[
             pltpu.VMEM((2, 2, chunk, width), BF16),
@@ -313,11 +417,18 @@
             pltpu.VMEM((steps, 2 * width, part), BF16),
             pltpu.VMEM((steps - 1, 2 * width, part), BF16),
             pltpu.VMEM((seq, min(SUB, chunk)), BF16),
-            sems((2, steps)),
-            sems((2, steps)),
-            sems((steps,)),
-            sems((steps,)),
-            sems((steps,)),
+            sems((steps, 2, 2)),
+            sems((2, steps, n_tensor)),
+            sems((4,)),
+            sems((steps,)),
+            sems((steps,)),
+            sems((steps,)),
+            sems((steps,)),
+            sems((steps,)),
+            sems((steps, 2)),
+            sems((steps, 2)),
+            sems((others, steps, 2)),
+            sems((others, steps, 2)),
             sems((others, steps)),
             sems((others, steps)),
             sems((steps,)),
@@ -333,16 +444,38 @@
         cost_estimate=pl.CostEstimate(
             flops=8 * seq * width * model, bytes_accessed=8 * model * width, transcendentals=0
         ),
-    )(kg, vg, kt, vt, hid, w_half)[:3]
+    )(kg, vg, kt, vt, hidden, hid_early, w_mine, w_below, w_above, w_beside)[:3]
 
 
 def on_device(mesh, hidden_in, queries, keys, values, out_grad, w_key, w_value, adam_state):
+    n_dp, n_tensor = mesh.shape["dp"], mesh.shape["tensor"]
+    steps = n_dp // 2
+    part = hidden_in.shape[1] // (2 * n_dp)
+    r, a = lax.axis_index("rep"), lax.axis_index("dp") // 2
+
+    early = []
+    for i in range(EARLY):
+        for owner in (1 - r, r):
+            first = (owner * n_dp + (a + 1 + i) % steps * 2) * part
+            early.append(lax.dynamic_slice_in_dim(hidden_in, first, 2 * part, 1))
+    early = jnp.stack(early).reshape(EARLY, 2, -1, 2 * part)
+    hid_early = jnp.stack(
+        [
+            lax.ppermute(early, "tensor", [(t, (t + 1 + k) % n_tensor) for t in range(n_tensor)])
+            for k in range(n_tensor - 1)
+        ]
+    )
+
+    w_mine = jnp.where(r == 0, w_key, w_value)
+    w_beside = lax.ppermute(w_mine, "dp", [(d, d ^ 1) for d in range(n_dp)])
+    w_below = lax.ppermute(w_mine, "dp", [(d, d + 2) for d in range(n_dp - 2)])
+    w_above = lax.ppermute(w_mine, "dp", [(d + 2, d) for d in range(n_dp - 2)])
     state_backup = lax.ppermute(adam_state, "rep", [(0, 1), (1, 0)])
-    hidden = lax.all_gather(hidden_in, "tensor", axis=0, tiled=True)
-    w_mine = jnp.where(lax.axis_index("rep") == 0, w_key, w_value)
-    w_half = lax.all_gather(w_mine, "dp", axis=0, tiled=True)
+
     query_grad, kg, vg, kt, vt = attention_grads(queries, keys, values, out_grad)
-    input_grad, key_weight_grad, value_weight_grad = tail(mesh, kg, vg, kt, vt, hidden, w_half)
+    input_grad, key_weight_grad, value_weight_grad = tail(
+        mesh, kg, vg, kt, vt, hidden_in, hid_early, w_mine, w_below, w_above, w_beside
+    )
     return (query_grad, input_grad, key_weight_grad, value_weight_grad, state_backup)
 
 

time: 399 us -> 381 us (0.955)
  waiting for transfers between devices: 186 us -> 0.01 us
  Pallas kernels: 176 us -> 351 us
  between operations: 14.1 us -> 0.8 us
  starting transfers between devices: 1.2 us -> 9.94 us
  local copies, waits for them, and re-layouts: 19.4 us -> 12.8 us
    all_gather x2 -> x0, waiting for transfers between devices: 186 us -> none  [the longest x1 126 us: on_device(): w_half = lax.all_gather(w_mine, 'dp', axis=0, tiled=True)]
    pallas_call x1, Pallas kernels: 139 us -> 313 us  [tail(): pl.pallas_call(functools.partial(tail_kernel, n_dp, n_tensor, EARLY), in_...]
    ppermute x0 -> x4, starting transfers between devices: none -> 9.87 us  [the longest x1 3.49 us: on_device(): w_below = lax.ppermute(w_mine, 'dp', [(d, d + 2) for d in range(n_dp - 2)])]
    unnamed x30 -> x14, local copies, waits for them, and re-layouts: 19.4 us -> 11.4 us
  transfers between devices with their start and end apart: 3 -> 5, of which waited for: 2 -> 0; matrix products, arithmetic and copies ran while one was open for 0% -> 1% of each run, Pallas kernels for 9% -> 93%
where the time goes in v2:
time: 381 us; the launch traced here: 376 us
  Pallas kernels  351 us (92%)
  local copies, waits for them, and re-layouts  12.8 us (3%)
  starting transfers between devices  9.94 us (3%)
    pallas_call x1, Pallas kernels, tail(): pl.pallas_call(functools.partial(tail_kernel, n_dp, n_tensor, EARLY), in_...  313 us
    pallas_call x1, Pallas kernels, attention_grads(): pl.pallas_call(attention_kernel, grid=(groups,), in_specs=[wide, narrow,...  38 us
    unnamed x14, local copies, waits for them, and re-layouts  11.4 us
  transfers between devices with their start and end apart: 5, of which 0 were waited for; matrix products, arithmetic and copies ran while one was open for 1% of the time, Pallas kernels for 93%

profile of v2, /device:TPU:8, one launch (start us, length us, event | category | flops | bytes accessed | tf_op | source)
XLA Modules:
  0.0 376.0 jit_solution(467041593668093989)
XLA Ops:
  0.6 0.0 copy-start
  0.7 0.1 collective-permute-start.4
  0.8 1.4 dynamic-slice_bitcast_fusion.1
  2.2 1.1 maximum_bitcast_fusion
  3.2 1.5 collective-permute-start
  4.7 0.0 copy-done.1
  4.7 0.1 broadcast_select_fusion.w_ref
  4.9 0.0 copy-start.2
  4.9 3.5 collective-permute-start.1
  8.4 3.3 collective-permute-start.2
  11.7 1.6 collective-permute-start.3
  13.3 38.0 %shard_map.137 = (bf16[512,4096]{1,0:T(8,128)(2,1)}, bf16[512,512]{1,0:T(8,128)(2,1)}, bf16[512,512]{1,0:T(8,128)(2,1)}, bf16[512,512]{1,0:T(8,128)(2,1)}, bf16[512,512]{1,0:T(8,128)(2,1)}) custom-call(bf16[512,4096]{1,0:T(8,128)(2,1)} %q_ref.1, bf16[512,512]{1,0:T(8,128)(2,1)} %k_ref.1, bf16[512,512]{1,0:T(8,128)(2,1)} %v_ref.1, bf16[512,4096]{1,0:T(8,128)(2,1)} %og_ref.1, ...), custom_call_target="tpu_custom_call" | custom-call | flops 10737418240 | bytes 15728640 | tf_op jit(solution)/shard_map/pallas_call | solution.py:86
  51.2 0.0 collective-permute-done
  51.2 0.0 collective-permute-done.1.w_below
  51.2 0.0 collective-permute-done.2.w_above
  51.3 0.0 collective-permute-done.3.w_beside
  51.3 313.3 %shard_map.138 = (bf16[256,8192]{1,0:T(8,128)(2,1)}, f32[512,512]{1,0:T(8,128)}, f32[512,512]{1,0:T(8,128)}, bf16[2,4,2,1024,512]{4,3,2,1,0:T(8,128)(2,1)}, bf16[1,4,2,256,1024]{4,3,2,1,0:T(8,128)(2,1)}) custom-call(bf16[512,512]{1,0:T(8,128)(2,1)} %get-tuple-element.14.kg_ref, bf16[512,512]{1,0:T(8,128)(2,1)} %get-tuple-element.15.vg_ref, ...), custom_call_target="tpu_custom_call" | custom-call | flops 17179869184 | bytes 33554432 | tf_op jit(solution)/shard_map/pallas_call | solution.py:396
  364.6 0.0 collective-permute-done.4
  364.6 0.0 copy-start.4
  364.6 0.0 copy-start.3
  364.6 4.8 %copy.19 = bf16[256,8192]{1,0:T(8,128)(2,1)} copy(bf16[256,8192]{1,0:T(8,128)(2,1)} %get-tuple-element.29) | data formatting | bytes 8388608
  369.4 1.0 copy.20
  370.4 1.0 copy.21
  371.3 4.6 %copy.22 = f32[2,2,512,512]{3,2,1,0:T(8,128)} copy(f32[2,2,512,512]{3,2,1,0:T(8,128)} %collective-permute-done.4) | data formatting | bytes 8388608
  (5 shorter events, 0.0 us)
Async XLA Ops:
  0.6 4.1 %copy-start = (bf16[1024,512]{1,0:T(8,128)(2,1)S(1)}, bf16[1024,512]{1,0:T(8,128)(2,1)}, u32[]{:S(2)}) copy-start(bf16[1024,512]{1,0:T(8,128)(2,1)} %param.15) | copy-start | bytes 3145732
  0.6 4.1 %copy-start.1 = (bf16[1024,512]{1,0:T(8,128)(2,1)S(1)}, bf16[1024,512]{1,0:T(8,128)(2,1)}, u32[]{:S(2)}) copy-start(bf16[1024,512]{1,0:T(8,128)(2,1)} %param.16) | copy-start | bytes 3145732
  0.7 363.9 %collective-permute-start.4 = (f32[2,2,512,512]{3,2,1,0:T(8,128)}, f32[2,2,512,512]{3,2,1,0:T(8,128)}, u32[]{:S(2)}, u32[]{:S(2)}) collective-permute-start(f32[2,2,512,512]{3,2,1,0:T(8,128)} %param.17), channel_id=1, source_target_pairs={{0,16},{16,0},{1,17},{17,1},{2,18},{18,2},{3,19},{19,3},{4,20},{20... | collective-permute-start | bytes 12582920 | tf_op jit(solution)/shard_map/ppermute | solution.py:473
  3.2 48.0 %collective-permute-start = (bf16[1,2,256,1024]{3,2,1,0:T(8,128)(2,1)}, bf16[1,2,256,1024]{3,2,1,0:T(8,128)(2,1)}, u32[]{:S(2)}, u32[]{:S(2)}) collective-permute-start(bf16[1,2,256,1024]{3,2,1,0:T(8,128)(2,1)} %maximum_bitcast_fusion), channel_id=1, source_target_pairs={{0,1},{1,0},{2,3},{3,2},{4,5},{5,4},{6,7},{7,6},{8,9},{9,8},{10,11... | collective-permute-start | bytes 3145736 | tf_op jit(solution)/shard_map/ppermute | solution.py:464
  4.9 46.4 %copy-start.2 = (bf16[1024,512]{1,0:T(8,128)(2,1)}, bf16[1024,512]{1,0:T(8,128)(2,1)S(1)}, u32[]{:S(2)}) copy-start(bf16[1024,512]{1,0:T(8,128)(2,1)S(1)} %broadcast_select_fusion.w_ref) | copy-start | bytes 3145732
  4.9 46.4 %collective-permute-start.1 = (bf16[1024,512]{1,0:T(8,128)(2,1)S(1)}, bf16[1024,512]{1,0:T(8,128)(2,1)}, u32[]{:S(2)}, u32[]{:S(2)}) collective-permute-start(bf16[1024,512]{1,0:T(8,128)(2,1)S(1)} %broadcast_select_fusion.w_ref), channel_id=1, source_target_pairs={{0,4},{2,6},{4,8},{6,10},{8,12},{10,14},{1,5},{3,7},{5,9},{7,11},{... | collective-permute-start | bytes 3145736 | tf_op jit(solution)/shard_map/ppermute | solution.py:471
  8.4 42.9 %collective-permute-start.2 = (bf16[1024,512]{1,0:T(8,128)(2,1)S(1)}, bf16[1024,512]{1,0:T(8,128)(2,1)}, u32[]{:S(2)}, u32[]{:S(2)}) collective-permute-start(bf16[1024,512]{1,0:T(8,128)(2,1)S(1)} %broadcast_select_fusion.w_ref), channel_id=1, source_target_pairs={{4,0},{6,2},{8,4},{10,6},{12,8},{14,10},{5,1},{7,3},{9,5},{11,7},{... | collective-permute-start | bytes 3145736 | tf_op jit(solution)/shard_map/ppermute | solution.py:472
  11.7 39.6 %collective-permute-start.3 = (bf16[1024,512]{1,0:T(8,128)(2,1)S(1)}, bf16[1024,512]{1,0:T(8,128)(2,1)}, u32[]{:S(2)}, u32[]{:S(2)}) collective-permute-start(bf16[1024,512]{1,0:T(8,128)(2,1)S(1)} %broadcast_select_fusion.w_ref), channel_id=1, source_target_pairs={{0,2},{2,0},{4,6},{6,4},{8,10},{10,8},{12,14},{14,12},{1,3},{3,1},... | collective-permute-start | bytes 3145736 | tf_op jit(solution)/shard_map/ppermute | solution.py:470
  364.6 4.8 %copy-start.4 = (f32[512,512]{1,0:T(8,128)S(1)}, f32[512,512]{1,0:T(8,128)}, u32[]{:S(2)}) copy-start(f32[512,512]{1,0:T(8,128)} %get-tuple-element.30) | copy-start | bytes 3145732
  364.6 5.8 %copy-start.3 = (f32[512,512]{1,0:T(8,128)S(1)}, f32[512,512]{1,0:T(8,128)}, u32[]{:S(2)}) copy-start(f32[512,512]{1,0:T(8,128)} %get-tuple-element.31) | copy-start | bytes 3145732

commit v3 on v2

--- a/solution.py
+++ b/solution.py
@@ -183,15 +183,18 @@
             for which in range(2)
         ]
 
+    def away(i):
+        return jnp.abs(near[i] - a)
+
     def take_line(i):
         if i >= 1:
 
-            @pl.when(jnp.abs(near[i] - a) >= 2)
+            @pl.when(away(i) >= 2)
             def _():
                 w_onward(i)[1].wait_recv()
 
             inside, copy = w_onward(i)
-            pl.when(inside)(copy.start)
+            pl.when(inside & (away(i) >= 2))(copy.start)
             w_sideways(i).start()
         w_swap(i, False).start()
 
@@ -228,6 +231,8 @@
         if i >= early:
             for k in range(others):
                 hid_send(mine, i, k).wait_recv()
+                if i + 1 < steps:
+                    hid_send(mine, i + 1, k).start()
         for copy in hid_load(mine, i):
             copy.start()
 
@@ -284,54 +289,79 @@
     pl.when(a >= 1)(enter(2, w_below, below, b).start)
     pl.when(a + 1 < steps)(enter(3, w_above, above, b).start)
     pl.semaphore_wait(barrier, len(peers))
-    for i in range(early, steps):
-        for mine in (False, True):
-            for k in range(others):
-                hid_send(mine, i, k).start()
+    for mine in (False, True):
+        for k in range(others):
+            hid_send(mine, early, k).start()
     enter(0, w_ref, a, b).wait()
     enter(1, w_beside, a, 1 - b).wait()
     pl.when(a >= 1)(enter(2, w_below, below, b).wait)
     pl.when(a + 1 < steps)(enter(3, w_above, above, b).wait)
+    for i in range(1, min(3, steps)):
+        inside, copy = w_onward(i)
+        pl.when(inside & (away(i) == 1))(copy.start)
     take_line(0)
     take_beside(0)
     take_line(1)
 
-    for i in range(steps + 2):
-        if i < steps:
-            hid_start(False, i)
-            if i >= 1:
-                take_beside(i)
-                if i + 1 < steps:
-                    take_line(i + 1)
-            hid_wait(False, i)
-            if i >= 2:
-                a_copy(i - 2).wait_send()
-            other_products(i)
-            a_copy(i).start()
-            hid_start(True, i)
-            w_swap(i, False).wait_recv()
-            w_swap(i, True).wait_recv()
-            for copy in w_load(i):
-                copy.start()
-        if 1 <= i <= steps:
-            done = i - 1
-            hid_wait(True, done)
-            a_copy(done).wait_recv()
-            own_products(done, 1 - b, y_send)
-            y_copy(done).start()
-            own_products(done, b, y_own)
-        if i < steps:
-            for copy in w_load(i):
-                copy.wait()
-            input_grads(i)
-            for k in range(others):
-                ig_copy(i, k).start()
+    def input_step(i):
+        w_swap(i, False).wait_recv()
+        w_swap(i, True).wait_recv()
+        for copy in w_load(i):
+            copy.start()
+        for copy in w_load(i):
+            copy.wait()
+        input_grads(i)
+
+    def input_send(i):
+        for k in range(others):
+            ig_copy(i, k).start()
+
+    def along_step(i):
+        y_copy(i).wait_recv()
+        if i < steps - 1:
+            y_own[i] = (y_own[i].astype(F32) + y_recv[i].astype(F32)).astype(BF16)
+            z_copy(i).start()
+
+    taken, made, summed = 1, 0, 0
+    for i in range(steps):
+        hid_start(False, i)
+        hid_wait(False, i)
         if i >= 2:
-            done = i - 2
-            y_copy(done).wait_recv()
-            if done < steps - 1:
-                y_own[done] = (y_own[done].astype(F32) + y_recv[done].astype(F32)).astype(BF16)
-                z_copy(done).start()
+            a_copy(i - 2).wait_send()
+        other_products(i)
+        a_copy(i).start()
+        hid_start(True, i)
+        if i % 2 == 0:
+            input_step(made)
+            made += 1
+        hid_wait(True, i)
+        a_copy(i).wait_recv()
+        own_products(i, 1 - b, y_send)
+        y_copy(i).start()
+        own_products(i, b, y_own)
+        if 1 <= i < steps - 1:
+            take_line(i + 1)
+        if i % 2 == 1:
+            take_beside(taken)
+            taken += 1
+        if i >= 3:
+            along_step(summed)
+            summed += 1
+    for i in range(made):
+        input_send(i)
+    while made < steps:
+        if taken <= made:
+            take_beside(taken)
+            taken += 1
+        input_step(made)
+        input_send(made)
+        made += 1
+        if summed < steps:
+            along_step(summed)
+            summed += 1
+    while summed < steps:
+        along_step(summed)
+        summed += 1
 
     ig_out = []
     for i in range(steps):

time: 381 us -> 377 us (0.990); the launches traced: 376 us -> 377 us
  no operation moved by 1% of the time
where the time goes in v3:
time: 377 us
  Pallas kernels  352 us (93%)
  local copies, waits for them, and re-layouts  12.8 us (3%)
  starting transfers between devices  9.94 us (3%)
    pallas_call x1, Pallas kernels, tail(): pl.pallas_call(functools.partial(tail_kernel, n_dp, n_tensor, EARLY), in_...  314 us
    pallas_call x1, Pallas kernels, attention_grads(): pl.pallas_call(attention_kernel, grid=(groups,), in_specs=[wide, narrow,...  38 us
    unnamed x14, local copies, waits for them, and re-layouts  11.4 us
  transfers between devices with their start and end apart: 5, of which 0 were waited for; matrix products, arithmetic and copies ran while one was open for 1% of the time, Pallas kernels for 93%

profile of v3, /device:TPU:8, one launch (start us, length us, event | category | flops | bytes accessed | tf_op | source)
XLA Modules:
  0.0 377.0 jit_solution(11398967737997173739)
XLA Ops:
  0.6 0.0 copy-start
  0.6 0.0 copy-start.1
  0.7 0.1 collective-permute-start.4
  0.8 1.4 dynamic-slice_bitcast_fusion.1
  2.2 1.1 maximum_bitcast_fusion
  3.2 1.5 collective-permute-start
  4.7 0.0 copy-done.1
  4.7 0.1 broadcast_select_fusion.w_ref
  4.9 0.0 copy-start.2
  4.9 3.5 collective-permute-start.1
  8.4 3.3 collective-permute-start.2
  11.7 1.6 collective-permute-start.3
  13.3 38.0 %shard_map.137 = (bf16[512,4096]{1,0:T(8,128)(2,1)}, bf16[512,512]{1,0:T(8,128)(2,1)}, bf16[512,512]{1,0:T(8,128)(2,1)}, bf16[512,512]{1,0:T(8,128)(2,1)}, bf16[512,512]{1,0:T(8,128)(2,1)}) custom-call(bf16[512,4096]{1,0:T(8,128)(2,1)} %q_ref.1, bf16[512,512]{1,0:T(8,128)(2,1)} %k_ref.1, bf16[512,512]{1,0:T(8,128)(2,1)} %v_ref.1, bf16[512,4096]{1,0:T(8,128)(2,1)} %og_ref.1, ...), custom_call_target="tpu_custom_call" | custom-call | flops 10737418240 | bytes 15728640 | tf_op jit(solution)/shard_map/pallas_call | solution.py:86
  51.2 0.0 collective-permute-done
  51.2 0.0 collective-permute-done.1.w_below
  51.2 0.0 collective-permute-done.2.w_above
  51.3 0.0 collective-permute-done.3.w_beside
  51.3 314.3 %shard_map.138 = (bf16[256,8192]{1,0:T(8,128)(2,1)}, f32[512,512]{1,0:T(8,128)}, f32[512,512]{1,0:T(8,128)}, bf16[2,4,2,1024,512]{4,3,2,1,0:T(8,128)(2,1)}, bf16[1,4,2,256,1024]{4,3,2,1,0:T(8,128)(2,1)}) custom-call(bf16[512,512]{1,0:T(8,128)(2,1)} %get-tuple-element.14.kg_ref, bf16[512,512]{1,0:T(8,128)(2,1)} %get-tuple-element.15.vg_ref, ...), custom_call_target="tpu_custom_call" | custom-call | flops 17179869184 | bytes 33554432 | tf_op jit(solution)/shard_map/pallas_call | solution.py:426
  365.5 0.0 collective-permute-done.4
  365.6 4.8 %copy.19 = bf16[256,8192]{1,0:T(8,128)(2,1)} copy(bf16[256,8192]{1,0:T(8,128)(2,1)} %get-tuple-element.29) | data formatting | bytes 8388608
  370.4 1.0 copy.20
  371.3 0.0 copy-done.3
  371.3 1.0 copy.21
  372.3 4.6 %copy.22 = f32[2,2,512,512]{3,2,1,0:T(8,128)} copy(f32[2,2,512,512]{3,2,1,0:T(8,128)} %collective-permute-done.4) | data formatting | bytes 8388608
  (5 shorter events, 0.0 us)
Async XLA Ops:
  0.6 4.1 %copy-start = (bf16[1024,512]{1,0:T(8,128)(2,1)S(1)}, bf16[1024,512]{1,0:T(8,128)(2,1)}, u32[]{:S(2)}) copy-start(bf16[1024,512]{1,0:T(8,128)(2,1)} %param.15) | copy-start | bytes 3145732
  0.6 4.1 %copy-start.1 = (bf16[1024,512]{1,0:T(8,128)(2,1)S(1)}, bf16[1024,512]{1,0:T(8,128)(2,1)}, u32[]{:S(2)}) copy-start(bf16[1024,512]{1,0:T(8,128)(2,1)} %param.16) | copy-start | bytes 3145732
  0.7 364.9 %collective-permute-start.4 = (f32[2,2,512,512]{3,2,1,0:T(8,128)}, f32[2,2,512,512]{3,2,1,0:T(8,128)}, u32[]{:S(2)}, u32[]{:S(2)}) collective-permute-start(f32[2,2,512,512]{3,2,1,0:T(8,128)} %param.17), channel_id=1, source_target_pairs={{0,16},{16,0},{1,17},{17,1},{2,18},{18,2},{3,19},{19,3},{4,20},{20... | collective-permute-start | bytes 12582920 | tf_op jit(solution)/shard_map/ppermute | solution.py:503
  3.2 48.0 %collective-permute-start = (bf16[1,2,256,1024]{3,2,1,0:T(8,128)(2,1)}, bf16[1,2,256,1024]{3,2,1,0:T(8,128)(2,1)}, u32[]{:S(2)}, u32[]{:S(2)}) collective-permute-start(bf16[1,2,256,1024]{3,2,1,0:T(8,128)(2,1)} %maximum_bitcast_fusion), channel_id=1, source_target_pairs={{0,1},{1,0},{2,3},{3,2},{4,5},{5,4},{6,7},{7,6},{8,9},{9,8},{10,11... | collective-permute-start | bytes 3145736 | tf_op jit(solution)/shard_map/ppermute | solution.py:494
  4.9 46.4 %copy-start.2 = (bf16[1024,512]{1,0:T(8,128)(2,1)}, bf16[1024,512]{1,0:T(8,128)(2,1)S(1)}, u32[]{:S(2)}) copy-start(bf16[1024,512]{1,0:T(8,128)(2,1)S(1)} %broadcast_select_fusion.w_ref) | copy-start | bytes 3145732
  4.9 46.4 %collective-permute-start.1 = (bf16[1024,512]{1,0:T(8,128)(2,1)S(1)}, bf16[1024,512]{1,0:T(8,128)(2,1)}, u32[]{:S(2)}, u32[]{:S(2)}) collective-permute-start(bf16[1024,512]{1,0:T(8,128)(2,1)S(1)} %broadcast_select_fusion.w_ref), channel_id=1, source_target_pairs={{0,4},{2,6},{4,8},{6,10},{8,12},{10,14},{1,5},{3,7},{5,9},{7,11},{... | collective-permute-start | bytes 3145736 | tf_op jit(solution)/shard_map/ppermute | solution.py:501
  8.4 42.9 %collective-permute-start.2 = (bf16[1024,512]{1,0:T(8,128)(2,1)S(1)}, bf16[1024,512]{1,0:T(8,128)(2,1)}, u32[]{:S(2)}, u32[]{:S(2)}) collective-permute-start(bf16[1024,512]{1,0:T(8,128)(2,1)S(1)} %broadcast_select_fusion.w_ref), channel_id=1, source_target_pairs={{4,0},{6,2},{8,4},{10,6},{12,8},{14,10},{5,1},{7,3},{9,5},{11,7},{... | collective-permute-start | bytes 3145736 | tf_op jit(solution)/shard_map/ppermute | solution.py:502
  11.7 39.6 %collective-permute-start.3 = (bf16[1024,512]{1,0:T(8,128)(2,1)S(1)}, bf16[1024,512]{1,0:T(8,128)(2,1)}, u32[]{:S(2)}, u32[]{:S(2)}) collective-permute-start(bf16[1024,512]{1,0:T(8,128)(2,1)S(1)} %broadcast_select_fusion.w_ref), channel_id=1, source_target_pairs={{0,2},{2,0},{4,6},{6,4},{8,10},{10,8},{12,14},{14,12},{1,3},{3,1},... | collective-permute-start | bytes 3145736 | tf_op jit(solution)/shard_map/ppermute | solution.py:500
  365.6 4.8 %copy-start.4 = (f32[512,512]{1,0:T(8,128)S(1)}, f32[512,512]{1,0:T(8,128)}, u32[]{:S(2)}) copy-start(f32[512,512]{1,0:T(8,128)} %get-tuple-element.30) | copy-start | bytes 3145732
  365.6 5.8 %copy-start.3 = (f32[512,512]{1,0:T(8,128)S(1)}, f32[512,512]{1,0:T(8,128)}, u32[]{:S(2)}) copy-start(f32[512,512]{1,0:T(8,128)} %get-tuple-element.31) | copy-start | bytes 3145732

commit v4 on v1

--- a/solution.py
+++ b/solution.py
@@ -96,7 +96,7 @@
             jax.ShapeDtypeStruct((kv_width, seq), BF16),
         ],
         scratch_shapes=[pltpu.VMEM((seq, HD), F32), pltpu.VMEM((seq, HD), F32)],
-        compiler_params=pltpu.CompilerParams(vmem_limit_bytes=40 * 2**20),
+        compiler_params=pltpu.CompilerParams(vmem_limit_bytes=62 * 2**20),
         cost_estimate=pl.CostEstimate(
             flops=10 * seq * seq * width,
             bytes_accessed=2 * (3 * seq * width + 6 * seq * kv_width),
@@ -338,7 +338,13 @@
 
 def on_device(mesh, hidden_in, queries, keys, values, out_grad, w_key, w_value, adam_state):
     state_backup = lax.ppermute(adam_state, "rep", [(0, 1), (1, 0)])
-    hidden = lax.all_gather(hidden_in, "tensor", axis=0, tiled=True)
+    n_tensor, t = mesh.shape["tensor"], lax.axis_index("tensor")
+    piece = hidden_in.shape[0]
+    hidden = jnp.zeros((n_tensor * piece, hidden_in.shape[1]), BF16)
+    hidden = lax.dynamic_update_slice_in_dim(hidden, hidden_in, t * piece, 0)
+    for k in range(1, n_tensor):
+        got = lax.ppermute(hidden_in, "tensor", [(s, (s + k) % n_tensor) for s in range(n_tensor)])
+        hidden = lax.dynamic_update_slice_in_dim(hidden, got, (t + n_tensor - k) % n_tensor * piece, 0)
     w_mine = jnp.where(lax.axis_index("rep") == 0, w_key, w_value)
     w_half = lax.all_gather(w_mine, "dp", axis=0, tiled=True)
     query_grad, kg, vg, kt, vt = attention_grads(queries, keys, values, out_grad)

time: 399 us -> 294 us (0.74)
  waiting for transfers between devices: 186 us -> 74.6 us
    all_gather x1, waiting for transfers between devices: 126 us -> 27.4 us  [on_device(): w_half = lax.all_gather(w_mine, 'dp', axis=0, tiled=True)]
    all_gather x1 -> x0, waiting for transfers between devices: 59.8 us -> none  [on_device(): hidden = lax.all_gather(hidden_in, 'tensor', axis=0, tiled=True)]
    ppermute x0 -> x1, waiting for transfers between devices: none -> 47.2 us  [on_device(): lax.ppermute(hidden_in, 'tensor', [(s, (s + k) % n_tensor) for s in range...]
    unnamed x30 -> x10, local copies, waits for them, and re-layouts: 19.4 us -> 11.4 us
    dynamic_update_slice x0 -> x2, local copies, waits for them, and re-layouts: none -> 6.81 us  [the longest x1 4.6 us: on_device(): lax.dynamic_update_slice_in_dim(hidden, got, (t + n_tensor - k) % n_tenso...]
    broadcast_in_dim x0 -> x1, local copies, waits for them, and re-layouts: none -> 4.24 us  [on_device(): hidden = jnp.zeros((n_tensor * piece, hidden_in.shape[1]), BF16)]
  transfers between devices with their start and end apart: 3 -> 3, of which waited for: 2 -> 2; matrix products, arithmetic and copies ran while one was open for 0% -> 4% of each run, Pallas kernels for 9% -> 13%
where the time goes in v4:
time: 294 us; the launch traced here: 292 us
  Pallas kernels  177 us (60%)
  waiting for transfers between devices  74.6 us (25%)
  local copies, waits for them, and re-layouts  22.4 us (8%)
  between operations  14.1 us (5%)
    pallas_call x1, Pallas kernels, tail(): pl.pallas_call(functools.partial(tail_kernel, n_dp, n_tensor), in_specs=[...  139 us
    ppermute x1, waiting for transfers between devices, on_device(): lax.ppermute(hidden_in, 'tensor', [(s, (s + k) % n_tensor) for s in range...  47.2 us
    pallas_call x1, Pallas kernels, attention_grads(): pl.pallas_call(attention_kernel, grid=(groups,), in_specs=[wide, narrow,...  38.1 us
    all_gather x1, waiting for transfers between devices, on_device(): w_half = lax.all_gather(w_mine, 'dp', axis=0, tiled=True)  27.4 us
    unnamed x10, local copies, waits for them, and re-layouts  11.4 us
  transfers between devices with their start and end apart: 3, of which 2 were waited for; matrix products, arithmetic and copies ran while one was open for 4% of the time, Pallas kernels for 13%

profile of v4, /device:TPU:8, one launch (start us, length us, event | category | flops | bytes accessed | tf_op | source)
XLA Modules:
  0.0 292.2 jit_solution(1833382053214393025)
XLA Ops:
  7.2 0.0 all-gather.2.cloned.1.call-start
  7.2 2.3 broadcast_select_fusion
  9.5 0.0 all-gather.2.cloned.1.call-update
  9.6 0.1 collective-permute-start.1
  9.6 1.6 collective-permute-start
  11.2 0.0 copy-start
  11.2 4.2 %broadcast_in_dim.3 = bf16[512,8192]{1,0:T(8,128)(2,1)} broadcast(bf16[]{:T(256)} %constant.27.clone.1), dimensions={} | broadcast | bytes 8388610 | tf_op jit(solution)/shard_map/broadcast_in_dim | solution.py:343
  15.4 0.0 copy-done
  15.4 2.2 constant_dynamic-update-slice_fusion.1
  17.7 38.1 %shard_map.137 = (bf16[512,4096]{1,0:T(8,128)(2,1)}, bf16[512,512]{1,0:T(8,128)(2,1)}, bf16[512,512]{1,0:T(8,128)(2,1)}, bf16[512,512]{1,0:T(8,128)(2,1)}, bf16[512,512]{1,0:T(8,128)(2,1)}) custom-call(bf16[512,4096]{1,0:T(8,128)(2,1)} %q_ref.1, bf16[512,512]{1,0:T(8,128)(2,1)} %k_ref.1, bf16[512,512]{1,0:T(8,128)(2,1)} %v_ref.1, bf16[512,4096]{1,0:T(8,128)(2,1)} %og_ref.1, ...), custom_call_target="tpu_custom_call" | custom-call | flops 10737418240 | bytes 15728640 | tf_op jit(solution)/shard_map/pallas_call | solution.py:86
  55.7 0.0 collective-permute-done.1
  55.7 47.2 %collective-permute-done = bf16[256,8192]{1,0:T(8,128)(2,1)} collective-permute-done((bf16[256,8192]{1,0:T(8,128)(2,1)}, bf16[256,8192]{1,0:T(8,128)(2,1)}, u32[]{:S(2)}, u32[]{:S(2)}) %collective-permute-start) | collective-permute-done | bytes 4194336 | tf_op jit(solution)/shard_map/ppermute | solution.py:346
  102.9 4.6 %constant_dynamic-update-slice_fusion.hid_ref = bf16[512,8192]{1,0:T(8,128)(2,1)} fusion(bf16[512,8192]{1,0:T(8,128)(2,1)} %constant_dynamic-update-slice_fusion.1, bf16[256,8192]{1,0:T(8,128)(2,1)} %collective-permute-done, s32[]{:T(128)S(6)} %select_n.23), kind=kLoop, calls=%fused_computation.1 | loop fusion | bytes 8388612 | tf_op jit(solution)/shard_map/dynamic_update_slice | solution.py:347
  107.5 27.4 %all-gather.2.cloned.1.call-done.w_ref = bf16[8192,512]{1,0:T(8,128)(2,1)} async-done(((bf16[1024,512]{1,0:T(8,128)(2,1)}), bf16[8192,512]{1,0:T(8,128)(2,1)}) %all-gather.2.cloned.1.call-update) | async-done | bytes 8388624 | tf_op jit(solution)/shard_map/all_gather | solution.py:349
  135.0 139.0 %shard_map.138 = (bf16[256,8192]{1,0:T(8,128)(2,1)}, f32[512,512]{1,0:T(8,128)}, f32[512,512]{1,0:T(8,128)}, bf16[8192,512]{1,0:T(8,128)(2,1)}) custom-call(bf16[512,512]{1,0:T(8,128)(2,1)} %get-tuple-element.14.kg_ref, bf16[512,512]{1,0:T(8,128)(2,1)} %get-tuple-element.15.vg_ref, bf16[512,512]{1,0:T(8,128)(2,1)} %get-tuple-element.16.kt_ref, ...), custom_call_target="tpu_custom_call" | custom-call | flops 17179869184 | bytes 33554432 | tf_op jit(solution)/shard_map/pallas_call | solution.py:293
  274.0 0.0 copy-start.2
  274.0 0.0 copy-start.1
  274.0 4.8 %copy.21 = bf16[256,8192]{1,0:T(8,128)(2,1)} copy(bf16[256,8192]{1,0:T(8,128)(2,1)} %get-tuple-element.27) | data formatting | bytes 8388608
  278.8 0.0 copy-done.2
  278.8 1.0 copy.22
  279.8 0.0 copy-done.1
  279.8 1.0 copy.23
  280.7 4.6 %copy.24 = f32[2,2,512,512]{3,2,1,0:T(8,128)} copy(f32[2,2,512,512]{3,2,1,0:T(8,128)} %collective-permute-done.1) | data formatting | bytes 8388608
Async XLA Ops:
  7.2 127.8 %all-gather.2.cloned.1.call-start = ((), (), s32[]{:S(2)}) async-start(), calls=%async_computation | async-start | bytes 9437184 | tf_op jit(solution)/shard_map/all_gather | solution.py:349
  9.6 46.2 %collective-permute-start.1 = (f32[2,2,512,512]{3,2,1,0:T(8,128)}, f32[2,2,512,512]{3,2,1,0:T(8,128)}, u32[]{:S(2)}, u32[]{:S(2)}) collective-permute-start(f32[2,2,512,512]{3,2,1,0:T(8,128)} %param.17), channel_id=1, source_target_pairs={{0,16},{16,0},{1,17},{17,1},{2,18},{18,2},{3,19},{19,3},{4,20},{20... | collective-permute-start | bytes 12582920 | tf_op jit(solution)/shard_map/ppermute | solution.py:340
  9.6 93.3 %collective-permute-start = (bf16[256,8192]{1,0:T(8,128)(2,1)}, bf16[256,8192]{1,0:T(8,128)(2,1)}, u32[]{:S(2)}, u32[]{:S(2)}) collective-permute-start(bf16[256,8192]{1,0:T(8,128)(2,1)} %param.10), channel_id=1, source_target_pairs={{0,1},{1,0},{2,3},{3,2},{4,5},{5,4},{6,7},{7,6},{8,9},{9,8},{10,11... | collective-permute-start | bytes 12582920 | tf_op jit(solution)/shard_map/ppermute | solution.py:346
  11.2 4.2 %copy-start = (bf16[256,8192]{1,0:T(8,128)(2,1)S(1)}, bf16[256,8192]{1,0:T(8,128)(2,1)}, u32[]{:S(2)}) copy-start(bf16[256,8192]{1,0:T(8,128)(2,1)} %param.10) | copy-start | bytes 12582916
  274.0 4.8 %copy-start.2 = (f32[512,512]{1,0:T(8,128)S(1)}, f32[512,512]{1,0:T(8,128)}, u32[]{:S(2)}) copy-start(f32[512,512]{1,0:T(8,128)} %get-tuple-element.28) | copy-start | bytes 3145732
  274.0 5.8 %copy-start.1 = (f32[512,512]{1,0:T(8,128)S(1)}, f32[512,512]{1,0:T(8,128)}, u32[]{:S(2)}) copy-start(f32[512,512]{1,0:T(8,128)} %get-tuple-element.29) | copy-start | bytes 3145732
Sparse Core Ops, SparseCore 0:
  10.7 124.2 all-gather.1
